TPU v7x, 32 devices: a whole 2x2x4 slice. The times are simulated.
32 devices in a mesh: shard: 8 (over y, x, core), rep: 4 (over z).
Axes of the slice: x: 2, y: 2, z: 4, core: 2. Of those that a mesh axis runs over, the one named last changes fastest.
Arguments:
- rows_in: bfloat16 [16384, 2048], P(('shard', 'rep')), may hold values from -6 to 6
- cotangent: bfloat16 [16384, 2048], P(('shard', 'rep')), may hold values from -6 to 6
- expert_counts: int32 [32, 2], P(('shard', 'rep')), may hold values from 0 to 512, as said below
- weights: bfloat16 [2048, 2, 1152], P('shard'), may hold values from -0.125 to 0.125
Outputs:
- rows_out: bfloat16 [16384, 2048], P(('shard', 'rep'))
- rows_grad: bfloat16 [16384, 2048], P(('shard', 'rep'))
- weight_grad: float32 [2048, 2, 1152], P('shard')
Inputs may be any that keep to these rules, and one draw needn't show every extreme that they name: `expert_counts`: on each device the experts' regions, each padded to a multiple of 128 rows, follow one another from row 0 and together fill at most 512 rows; some device fills all 512; one expert on some device holds all 512 rows.
All inputs are finite; a program needn't handle non-finite values.
Results may differ from a plain program's by a relative error of at most 0.0095.
Values may be sent and summed in bfloat16 or wider, within the bound.
A program may use at most 128 MiB of HBM per device.

v0:
```python
import jax
import jax.numpy as jnp
from jax import lax
from jax.sharding import PartitionSpec as P

BLOCK = 128


def expert_block(inputs, upstream, expert_slab):
    hidden_width = expert_slab.shape[1] // 3
    gate_up = expert_slab[:, : 2 * hidden_width]
    down_t = expert_slab[:, 2 * hidden_width :]
    project = jnp.dot(inputs, gate_up, preferred_element_type=jnp.float32)
    gate_pre = project[:, :hidden_width]
    up_pre = project[:, hidden_width:]
    gate_sigmoid = jax.nn.sigmoid(gate_pre)
    active = gate_pre * gate_sigmoid
    hidden = (active * up_pre).astype(jnp.bfloat16)
    output = lax.dot_general(
        hidden, down_t, (((1,), (1,)), ((), ())), preferred_element_type=jnp.float32
    ).astype(jnp.bfloat16)
    hidden_grad = jnp.dot(upstream, down_t, preferred_element_type=jnp.float32)
    down_grad = lax.dot_general(
        upstream, hidden, (((0,), (0,)), ((), ())), preferred_element_type=jnp.float32
    )
    gate_grad = hidden_grad * up_pre * gate_sigmoid * (1.0 + gate_pre * (1.0 - gate_sigmoid))
    up_grad = hidden_grad * active
    joint_grad = jnp.concatenate([gate_grad, up_grad], axis=1).astype(jnp.bfloat16)
    proj_grad = lax.dot_general(
        inputs, joint_grad, (((0,), (0,)), ((), ())), preferred_element_type=jnp.float32
    )
    input_grad = lax.dot_general(
        joint_grad, gate_up, (((1,), (1,)), ((), ())), preferred_element_type=jnp.float32
    ).astype(jnp.bfloat16)
    return (output, input_grad, jnp.concatenate([proj_grad, down_grad], axis=1))


def alive_rows(counts, total_rows):
    padded = (counts + BLOCK - 1) // BLOCK * BLOCK
    starts = jnp.cumsum(padded) - padded
    position = jnp.arange(total_rows, dtype=jnp.int32)
    inside = (position[:, None] >= starts[None, :]) & (
        position[:, None] < (starts + counts)[None, :]
    )
    return (jnp.any(inside, axis=1), padded, starts)


def run_expert(expert_slab, inputs, upstream, start_row, nblocks, outputs, input_grads):

    def block_step(block_index, state):
        outputs, input_grads, grad_total = state
        row_begin = start_row + block_index * BLOCK
        block_in = lax.dynamic_slice_in_dim(inputs, row_begin, BLOCK, 0)
        block_up = lax.dynamic_slice_in_dim(upstream, row_begin, BLOCK, 0)
        output, input_grad, grad_piece = expert_block(block_in, block_up, expert_slab)
        outputs = lax.dynamic_update_slice_in_dim(outputs, output, row_begin, 0)
        input_grads = lax.dynamic_update_slice_in_dim(input_grads, input_grad, row_begin, 0)
        return (outputs, input_grads, grad_total + grad_piece)

    start_grad = jnp.zeros(expert_slab.shape, jnp.float32)
    return lax.fori_loop(jnp.int32(0), nblocks, block_step, (outputs, input_grads, start_grad))


def reduce_grads(grads):
    partial_sum = lax.psum_scatter(grads, "shard", scatter_dimension=0, tiled=True)
    return lax.psum(partial_sum.astype(jnp.bfloat16), "rep").astype(jnp.float32)


def local(rows_in, cotangent, expert_counts, weights):
    counts = expert_counts[0]
    alive, padded, starts = alive_rows(counts, rows_in.shape[0])
    inputs = jnp.where(alive[:, None], rows_in, jnp.zeros_like(rows_in))
    upstream = jnp.where(alive[:, None], cotangent, jnp.zeros_like(cotangent))
    outputs = jnp.zeros_like(rows_in)
    input_grads = jnp.zeros_like(rows_in)
    experts = weights.shape[1]
    pieces = []
    gathered = lax.all_gather(weights, "shard", axis=0, tiled=True)
    for expert in range(experts):
        outputs, input_grads, grad_total = run_expert(
            gathered[:, expert],
            inputs,
            upstream,
            starts[expert],
            padded[expert] // BLOCK,
            outputs,
            input_grads,
        )
        pieces.append(grad_total)
    reduced = reduce_grads(jnp.stack(pieces, axis=1))
    return (outputs, input_grads, reduced)


def solution(mesh):
    in_specs = (
        P(("shard", "rep"), None),
        P(("shard", "rep"), None),
        P(("shard", "rep"), None),
        P("shard", None, None),
    )
    out_specs = (P(("shard", "rep"), None), P(("shard", "rep"), None), P("shard", None, None))
    return jax.shard_map(local, mesh=mesh, in_specs=in_specs, out_specs=out_specs, check_vma=False)
```

profile of v0, /device:TPU:0, one launch (start us, length us, event | category | flops | bytes accessed | tf_op | source)
XLA Modules:
  0.0 419.8 jit_solution(724378085125685798)
XLA Ops:
  7.2 2.4 copy.14
  15.9 3.9 broadcast_select_fusion
  19.8 52.3 %all-gather.2.cloned.1.call-done = bf16[2048,2,1152]{2,0,1:T(8,128)(2,1)} async-done(((bf16[256,2,1152]{2,0,1:T(8,128)(2,1)}), bf16[2048,2,1152]{2,0,1:T(8,128)(2,1)}) %all-gather.2.cloned.1.call-update) | async-done | bytes 9437200 | tf_op jit(solution)/shard_map/all_gather | solution.py:78
  72.0 8.2 %slice_bitcast_fusion = (bf16[2048,1152]{1,0:T(8,128)(2,1)}, bf16[2048,1152]{1,0:T(8,128)(2,1)}) fusion(bf16[2048,2,1152]{2,0,1:T(8,128)(2,1)} %all-gather.2.cloned.1.call-done), kind=kLoop, calls=%fused_computation.57 | loop fusion | bytes 18874368 | tf_op jit(solution)/shard_map/squeeze | solution.py:81
  83.3 4.8 %broadcast.131.clone = f32[2048,1152]{0,1:T(8,128)} broadcast(f32[]{:T(128)} %constant.62.clone.1), dimensions={} | broadcast | bytes 9437188 | tf_op jit(solution)/shard_map/broadcast.12
  88.2 24.6 %while.28 = (s32[]{:T(128)}, bf16[512,2048]{1,0:T(8,128)(2,1)}, bf16[512,2048]{1,0:T(8,128)(2,1)}, f32[2048,1152]{0,1:T(8,128)}, s32[]{:T(128)}, /*index=5*/s32[...) while((s32[]{:T(128)}, bf16[512,2048]{1,0:T(8,128)(2,1)}, ...), condition=%wide.region_3.4_spmd, body=%wide.region_2.3_spmd.sunk | while | flops 1818705920 | bytes 72974568 | solution.py:61
  88.9 2.6 fusion.87
  95.4 3.8 dynamic_update_slice.17
  99.2 3.8 dynamic_update_slice.16
  105.7 7.0 %maximum_add_fusion.4 = f32[2048,1152]{0,1:T(8,128)} fusion(f32[2048,1152]{0,1:T(8,128)} %get-tuple-element.311, f32[2048,384]{0,1:T(8,128)S(1)} %fusion.89, f32[2048,768]{0,1:T(8,128)S(1)} %fusion.90), kind=kLoop, calls=%fused_computation.clone.1 | loop fusion | flops 4718592 | bytes 28311552 | tf_op jit(solution)/shard_map/while/body/add | solution.py:58
  112.8 9.6 %copy.15 = f32[2048,1152]{1,0:T(8,128)} copy(f32[2048,1152]{0,1:T(8,128)} %get-tuple-element.107) | data formatting | bytes 18874368 | tf_op jit(solution)/shard_map/while | solution.py:61
  122.4 4.8 %broadcast.131 = f32[2048,1152]{0,1:T(8,128)} broadcast(f32[]{:T(128)} %constant.62.clone.1), dimensions={} | broadcast | bytes 9437188 | tf_op jit(solution)/shard_map/broadcast.12
  127.2 24.5 %while.29 = (s32[]{:T(128)}, bf16[512,2048]{1,0:T(8,128)(2,1)}, bf16[512,2048]{1,0:T(8,128)(2,1)}, f32[2048,1152]{0,1:T(8,128)}, s32[]{:T(128)}, /*index=5*/s32[...) while((s32[]{:T(128)}, bf16[512,2048]{1,0:T(8,128)(2,1)}, ...), condition=%wide.region_5.6_spmd, body=%wide.region_4.5_spmd.sunk | while | flops 1818705920 | bytes 72974568 | solution.py:61
  127.9 2.6 fusion.99
  134.4 3.8 dynamic_update_slice.19
  138.2 3.8 dynamic_update_slice.18
  142.0 1.7 fusion.101
  144.7 7.0 %maximum_add_fusion.5 = f32[2048,1152]{0,1:T(8,128)} fusion(f32[2048,1152]{0,1:T(8,128)} %get-tuple-element.350, f32[2048,384]{0,1:T(8,128)S(1)} %fusion.101, f32[2048,768]{0,1:T(8,128)S(1)} %fusion.102), kind=kLoop, calls=%fused_computation.28.clone.1 | loop fusion | flops 4718592 | bytes 28311552 | tf_op jit(solution)/shard_map/while/body/add | solution.py:58
  151.8 9.7 %copy.16 = f32[2048,1152]{1,0:T(8,128)} copy(f32[2048,1152]{0,1:T(8,128)} %get-tuple-element.108) | data formatting | bytes 18874368 | tf_op jit(solution)/shard_map/while | solution.py:61
  161.5 14.5 %pad_maximum_fusion.6 = f32[2048,2,1152]{2,0,1:T(8,128)} fusion(f32[2048,1,1152]{2,0,1:T(8,128)} %bitcast.52, f32[2048,1,1152]{2,0,1:T(8,128)} %bitcast.51), kind=kLoop, calls=%fused_computation.56 | loop fusion | flops 4718592 | bytes 37748736 | tf_op jit(solution)/shard_map/stack | solution.py:90
  176.0 174.5 %reduce-scatter.2.cloned.1.call-done = f32[256,2,1152]{2,0,1:T(8,128)} async-done(((f32[2048,2,1152]{2,0,1:T(8,128)}), f32[256,2,1152]{2,0,1:T(8,128)}) %reduce-scatter.2.cloned.1.call-update) | async-done | bytes 2359312 | tf_op jit(solution)/shard_map/reduce_scatter | solution.py:65
  350.5 2.8 convert_element_type.26
  353.3 56.1 %all-reduce.2.cloned.1.call-done = bf16[256,2,1152]{2,0,1:T(8,128)(2,1)} async-done(((bf16[256,2,1152]{2,0,1:T(8,128)(2,1)}), bf16[256,2,1152]{2,0,1:T(8,128)(2,1)}) %all-reduce.2.cloned.1.call-update) | async-done | bytes 1179664 | tf_op jit(solution)/shard_map/psum | solution.py:66
  409.4 3.9 copy.17
  (29 shorter events, 15.8 us)
Async XLA Ops:
  7.2 2.5 copy-start.2
  7.2 64.9 %all-gather.2.cloned.1.call-start = ((), (), s32[]{:S(2)}) async-start(), calls=%async_computation.1 | async-start | bytes 10616832 | tf_op jit(solution)/shard_map/all_gather | solution.py:78
  9.7 340.8 %reduce-scatter.2.cloned.1.call-start = ((), (), s32[]{:S(2)}) async-start(), calls=%async_computation.2 | async-start | bytes 21233664 | tf_op jit(solution)/shard_map/reduce_scatter | solution.py:65
  88.9 3.3 copy-start.1
  127.8 3.3 copy-start
  175.9 233.5 %all-reduce.2.cloned.1.call-start = ((), (), s32[]{:S(2)}) async-start(), calls=%async_computation.3 | async-start | bytes 2359296 | tf_op jit(solution)/shard_map/psum | solution.py:66
Sparse Core Ops, SparseCore 0:
  10.5 61.5 all-gather.1
  176.1 174.3 reduce-scatter.1
  353.5 55.9 all-reduce.1
where the time goes:
time: 421 us; the launch traced here: 420 us
  waiting for transfers between devices  283 us (67%)
  local copies, waits for them, and re-layouts  63.7 us (15%)
  other arithmetic  35.5 us (8%)
  between operations  19 us (5%)
  matrix products  17.2 us (4%)
    reduce_scatter x1, waiting for transfers between devices, reduce_grads(): lax.psum_scatter(grads, 'shard', scatter_dimension=0, tiled=True)  174 us
    psum x1, waiting for transfers between devices, reduce_grads(): return lax.psum(partial_sum.astype(jnp.bfloat16), 'rep').astype(jnp.float32)  56.1 us
    all_gather x1, waiting for transfers between devices, local(): gathered = lax.all_gather(weights, 'shard', axis=0, tiled=True)  52.3 us
    while x2, local copies, waits for them, and re-layouts, run_expert(): lax.fori_loop(jnp.int32(0), nblocks, block_step, (outputs, input_grads, s...  19.3 us
    another operation x1, other arithmetic, local(): reduced = reduce_grads(jnp.stack(pieces, axis=1))  14.5 us
    add x2, other arithmetic, block_step(): return (outputs, input_grads, grad_total + grad_piece)  14 us
    another operation x4, local copies, waits for them, and re-layouts  12.8 us
  transfers between devices with their start and end apart: 3, of which 3 were waited for; matrix products, arithmetic and copies ran while one was open for 1% of the time, Pallas kernels for 0%

commit v1 on v0

v1 whole, which is shorter than its diff:
```python
import functools

import jax
import jax.numpy as jnp
from jax import lax
from jax.experimental import pallas as pl
from jax.experimental.pallas import tpu as pltpu
from jax.sharding import PartitionSpec as P

BLOCK = 128
INNER = 8
MESH = pl.DeviceIdType.MESH
BF16, F32 = jnp.bfloat16, jnp.float32


def flip(index, bit):
    return index + bit - 2 * bit * lax.rem(lax.div(index, bit), 2)


def dot(a, b, dims):
    return lax.dot_general(a, b, (dims, ((), ())), preferred_element_type=F32)


NN, NT, TN = ((1,), (0,)), ((1,), (1,)), ((0,), (0,))


def kernel(
    counts_ref, x_ref, dy_ref, w_ref,
    out_ref, grad_ref, wg_ref,
    w_all, pre, hgrad, hid, joint,
    core_out, core_in, first_out, first_in, second_out, second_in, acc,
    z_out, z_in, z_peer, z_fin,
    w_sem, ag_send, ag_recv, core_send, core_recv, xy_send, xy_recv, z_send, z_recv,
):
    rows = x_ref.shape[0]
    experts, feat, width = w_ref.shape
    ff = width // 3
    shard = lax.axis_index("shard")
    rep = lax.axis_index("rep")
    local = lax.rem(shard, INNER)
    to_core, to_x, to_y = ((flip(shard, b), rep) for b in (1, 2, 4))
    z_pair, z_mirror = (shard, flip(rep, 1)), (shard, 3 - rep)
    inner_z = jnp.logical_or(rep == 1, rep == 2)
    partner = flip(local, 1)
    near = [local, flip(local, 2), flip(local, 4), flip(flip(local, 2), 4)]
    far = [partner, flip(partner, 2), flip(partner, 4), flip(flip(partner, 2), 4)]

    load = pltpu.make_async_copy(w_ref, w_all.at[local], w_sem)
    load.start()
    barrier = pltpu.get_barrier_semaphore()
    for other in (to_core, to_x, to_y, z_pair, z_mirror):
        pl.semaphore_signal(barrier, inc=1, device_id=other, device_id_type=MESH)
    load.wait()
    pl.semaphore_wait(barrier, 5)

    def share(k, member, e, device):
        block = w_all.at[member, e]
        return pltpu.make_async_remote_copy(
            src_ref=block, dst_ref=block, send_sem=ag_send.at[k], recv_sem=ag_recv.at[k],
            device_id=device, device_id_type=MESH,
        )

    gather = [
        share(0, near[0], 0, to_x), share(1, near[0], 1, to_x),
        share(2, near[0], 0, to_y), share(3, near[0], 1, to_y),
        share(4, near[1], 0, to_y), share(5, near[2], 1, to_x),
    ] + [share(6 + 2 * d + e, near[d], e, to_core) for d in range(4) for e in range(2)]
    for k in (0, 3, 6, 7, 1, 2):
        gather[k].start()

    position = lax.broadcasted_iota(jnp.int32, (rows, 1), 0)
    masks, start = [], jnp.int32(0)
    for e in range(experts):
        count = counts_ref[0, e]
        masks.append((position >= start) & (position < start + count))
        start = start + lax.div(count + (BLOCK - 1), BLOCK) * BLOCK

    def columns(member):
        return pl.ds(pl.multiple_of(member * feat, 128), feat)

    def project(member, first=False):
        x = x_ref[:, columns(member)]
        dy = dy_ref[:, columns(member)]
        zero = jnp.zeros_like(x)
        xs = [jnp.where(m, x, zero) for m in masks]
        dys = [jnp.where(m, dy, zero) for m in masks]
        p = sum(dot(xs[e], w_all[member, e, :, : 2 * ff], NN) for e in range(experts))
        h = sum(dot(dys[e], w_all[member, e, :, 2 * ff :], NN) for e in range(experts))
        if first:
            pre[...] = p
            hgrad[...] = h
        else:
            pre[...] += p
            hgrad[...] += h

    project(near[0], True)
    gather[6].wait_recv()
    gather[7].wait_recv()
    project(far[0])
    gather[0].wait_recv()
    gather[4].start()
    gather[8].start()
    gather[3].wait_recv()
    gather[5].start()
    gather[11].start()
    gather[1].wait_recv()
    gather[9].start()
    gather[2].wait_recv()
    gather[10].start()
    project(near[1])
    project(near[2])
    gather[8].wait_recv()
    gather[9].wait_recv()
    project(far[1])
    gather[10].wait_recv()
    gather[11].wait_recv()
    project(far[2])
    gather[4].wait_recv()
    gather[12].start()
    gather[5].wait_recv()
    gather[13].start()
    project(near[3])
    gather[12].wait_recv()
    gather[13].wait_recv()
    project(far[3])

    def activate(i, carry):
        at = pl.ds(pl.multiple_of(i * BLOCK, BLOCK), BLOCK)
        a, b, g = pre[at, :ff], pre[at, ff:], hgrad[at, :]
        s = jax.nn.sigmoid(a)
        active = a * s
        hidden = (active * b).astype(BF16)
        ga = (g * b * s * (1.0 + a * (1.0 - s))).astype(BF16)
        gb = (g * active).astype(BF16)
        place = lax.broadcasted_iota(jnp.int32, (BLOCK, 1), 0) + i * BLOCK
        begin = jnp.int32(0)
        for e in range(experts):
            count = counts_ref[0, e]
            keep = (place >= begin) & (place < begin + count)
            begin = begin + lax.div(count + (BLOCK - 1), BLOCK) * BLOCK
            zero = jnp.zeros_like(hidden)
            hid[e, at, :] = jnp.where(keep, hidden, zero)
            joint[e, at, :ff] = jnp.where(keep, ga, zero)
            joint[e, at, ff:] = jnp.where(keep, gb, zero)
        return carry

    lax.fori_loop(0, rows // BLOCK, activate, 0)

    def terms(member, e):
        at = columns(member)
        return (
            (slice(0, 2 * ff), dot(x_ref[:, at], joint[e], TN)),
            (slice(2 * ff, width), dot(dy_ref[:, at], hid[e], TN)),
        )

    def swap(d, e):
        return pltpu.make_async_remote_copy(
            src_ref=core_out.at[d, e], dst_ref=core_in.at[d, e],
            send_sem=core_send.at[d, e], recv_sem=core_recv.at[d, e],
            device_id=to_core, device_id_type=MESH,
        )

    def to_partner(d, e):
        for cols, value in terms(far[d], e):
            core_out[d, e, :, cols] = value.astype(BF16)
        swap(d, e).start()

    def step(k, src, dst, device):
        return pltpu.make_async_remote_copy(
            src_ref=src, dst_ref=dst, send_sem=xy_send.at[k], recv_sem=xy_recv.at[k],
            device_id=device, device_id_type=MESH,
        )

    first = [step(k, first_out.at[k], first_in.at[k], (to_x, to_y)[k % 2]) for k in range(4)]
    second = [step(4 + k, second_out.at[k], second_in.at[k], (to_y, to_x)[k]) for k in range(2)]

    def send_first(k, d, e):
        swap(d, e).wait_recv()
        for cols, value in terms(near[d], e):
            first_out[k, :, cols] = (value + core_in[d, e, :, cols].astype(F32)).astype(BF16)
        first[k].start()

    def keep_sum(k, d, e):
        swap(d, e).wait_recv()
        for cols, value in terms(near[d], e):
            acc[k, :, cols] = value + core_in[d, e, :, cols].astype(F32)

    def rows_of(member, carry):
        at = columns(member)
        out_ref[:, at] = sum(
            dot(hid[e], w_all[member, e, :, 2 * ff :], NT) for e in range(experts)
        ).astype(BF16)
        grad_ref[:, at] = sum(
            dot(joint[e], w_all[member, e, :, : 2 * ff], NT) for e in range(experts)
        ).astype(BF16)
        return carry

    to_partner(3, 0)
    to_partner(3, 1)
    send_first(0, 3, 0)
    send_first(1, 3, 1)
    to_partner(1, 0)
    to_partner(2, 1)
    send_first(2, 1, 0)
    send_first(3, 2, 1)
    to_partner(2, 0)
    to_partner(1, 1)
    to_partner(0, 0)
    to_partner(0, 1)
    keep_sum(0, 2, 0)
    keep_sum(1, 1, 1)
    keep_sum(2, 0, 0)
    keep_sum(3, 0, 1)
    for k in range(2):
        first[k].wait_recv()
        second_out[k] = (acc[k] + first_in[k].astype(F32)).astype(BF16)
        second[k].start()
    lax.fori_loop(0, INNER, rows_of, 0)
    for k in range(2):
        first[2 + k].wait_recv()
        acc[2 + k] += first_in[2 + k].astype(F32)

    def hop(j, k, src, dst, device):
        return pltpu.make_async_remote_copy(
            src_ref=src, dst_ref=dst, send_sem=z_send.at[j, k], recv_sem=z_recv.at[j, k],
            device_id=device, device_id_type=MESH,
        )

    half = feat // 2
    pieces = 2 * experts
    inward = [hop(0, k, z_out.at[k], z_in.at[k], z_pair) for k in range(pieces)]
    across = [hop(1, k, z_out.at[k], z_peer.at[k], z_mirror) for k in range(pieces)]
    outward = [hop(2, k, z_fin.at[k], z_fin.at[k], z_pair) for k in range(pieces)]

    for k in range(pieces):
        e, part = k // 2, slice((k % 2) * half, (k % 2 + 1) * half)
        if k % 2 == 0:
            second[e].wait_recv()

        @pl.when(jnp.logical_not(inner_z))
        def _():
            z_out[k] = (acc[2 + e, part] + second_in[e, part].astype(F32)).astype(BF16)
            inward[k].start()

        @pl.when(inner_z)
        def _():
            acc[2 + e, part] += second_in[e, part].astype(F32)

    @pl.when(inner_z)
    def _():
        for k in range(pieces):
            e, part = k // 2, slice((k % 2) * half, (k % 2 + 1) * half)
            inward[k].wait_recv()
            z_out[k] = (acc[2 + e, part] + z_in[k].astype(F32)).astype(BF16)
            across[k].start()
        for k in range(pieces):
            e, part = k // 2, slice((k % 2) * half, (k % 2 + 1) * half)
            across[k].wait_recv()
            z_fin[k] = (z_out[k].astype(F32) + z_peer[k].astype(F32)).astype(BF16)
            outward[k].start()
            wg_ref[e, part] = z_fin[k].astype(F32)
        for k in range(pieces):
            across[k].wait_send()
            outward[k].wait_send()

    @pl.when(jnp.logical_not(inner_z))
    def _():
        for k in range(pieces):
            e, part = k // 2, slice((k % 2) * half, (k % 2 + 1) * half)
            outward[k].wait_recv()
            wg_ref[e, part] = z_fin[k].astype(F32)
        for k in range(pieces):
            inward[k].wait_send()

    for copy in gather + first + second + [swap(d, e) for d in range(4) for e in range(experts)]:
        copy.wait_send()


def local(spread, rows_in, cotangent, expert_counts, weights):
    rows, model = rows_in.shape
    own, experts, width = weights.shape
    ff = width // 3
    feat = own * spread

    def regroup(v, a, b):
        return v if spread == 1 else v.reshape(rows, a, b, own).swapaxes(1, 2).reshape(rows, model)

    w = weights.swapaxes(0, 1)
    if spread > 1:
        peers = [[h * INNER + m for h in range(spread)] for m in range(INNER)]
        w = lax.all_gather(w, "shard", axis=1, tiled=True, axis_index_groups=peers)

    vmem = pl.BlockSpec(memory_space=pltpu.VMEM)
    dma = pltpu.SemaphoreType.DMA
    block = (feat, width)
    rows_out, rows_grad, wg = pl.pallas_call(
        kernel,
        out_shape=(
            jax.ShapeDtypeStruct((rows, model), BF16),
            jax.ShapeDtypeStruct((rows, model), BF16),
            jax.ShapeDtypeStruct((experts, feat, width), F32),
        ),
        in_specs=[
            pl.BlockSpec(memory_space=pltpu.SMEM), vmem, vmem,
            pl.BlockSpec(memory_space=pl.ANY),
        ],
        out_specs=(vmem, vmem, vmem),
        scratch_shapes=[
            pltpu.VMEM((INNER, experts, *block), BF16),
            pltpu.VMEM((rows, 2 * ff), F32),
            pltpu.VMEM((rows, ff), F32),
            pltpu.VMEM((experts, rows, ff), BF16),
            pltpu.VMEM((experts, rows, 2 * ff), BF16),
            pltpu.VMEM((4, experts, *block), BF16),
            pltpu.VMEM((4, experts, *block), BF16),
            pltpu.VMEM((4, *block), BF16),
            pltpu.VMEM((4, *block), BF16),
            pltpu.VMEM((2, *block), BF16),
            pltpu.VMEM((2, *block), BF16),
            pltpu.VMEM((4, *block), F32),
            pltpu.VMEM((2 * experts, feat // 2, width), BF16),
            pltpu.VMEM((2 * experts, feat // 2, width), BF16),
            pltpu.VMEM((2 * experts, feat // 2, width), BF16),
            pltpu.VMEM((2 * experts, feat // 2, width), BF16),
            dma,
            dma((14,)), dma((14,)),
            dma((4, experts)), dma((4, experts)),
            dma((6,)), dma((6,)),
            dma((3, 2 * experts)), dma((3, 2 * experts)),
        ],
        compiler_params=pltpu.CompilerParams(
            collective_id=0, has_side_effects=True, vmem_limit_bytes=62 * 1024 * 1024 - 1024 * 1024
        ),
        cost_estimate=pl.CostEstimate(
            flops=12 * rows * model * experts * width // 3 * 3, bytes_accessed=32 << 20,
            transcendentals=rows * ff,
        ),
    )(expert_counts, regroup(rows_in, spread, INNER), regroup(cotangent, spread, INNER), w)
    if spread > 1:
        wg = lax.psum_scatter(
            wg, "shard", scatter_dimension=1, tiled=True, axis_index_groups=peers
        )
    return regroup(rows_out, INNER, spread), regroup(rows_grad, INNER, spread), wg.swapaxes(0, 1)


def solution(mesh):
    rows_spec = P(("shard", "rep"), None)
    weight_spec = P("shard", None, None)
    return jax.shard_map(
        functools.partial(local, mesh.shape["shard"] // INNER),
        mesh=mesh,
        in_specs=(rows_spec, rows_spec, rows_spec, weight_spec),
        out_specs=(rows_spec, rows_spec, weight_spec),
        check_vma=False,
    )
```

time: 421 us -> 162 us (0.38)
  waiting for transfers between devices: 283 us -> 0 us
  Pallas kernels: 0 us -> 150 us
  local copies, waits for them, and re-layouts: 63.7 us -> 11.1 us
  other arithmetic: 35.5 us -> 0 us
  between operations: 19 us -> 0.65 us
  matrix products: 17.2 us -> 0 us
    reduce_scatter x1 -> x0, waiting for transfers between devices: 174 us -> none  [reduce_grads(): lax.psum_scatter(grads, 'shard', scatter_dimension=0, tiled=True)]
    pallas_call x0 -> x1, Pallas kernels: none -> 150 us  [local(): pl.pallas_call(kernel, out_shape=(jax.ShapeDtypeStruct((rows, model), BF1...]
    psum x1 -> x0, waiting for transfers between devices: 56.1 us -> none  [reduce_grads(): return lax.psum(partial_sum.astype(jnp.bfloat16), 'rep').astype(jnp.float32)]
    all_gather x1 -> x0, waiting for transfers between devices: 52.3 us -> none  [local(): gathered = lax.all_gather(weights, 'shard', axis=0, tiled=True)]
    while x6 -> x0, local copies, waits for them, and re-layouts: 20.6 us -> none  [the longest x2 19.3 us: run_expert(): lax.fori_loop(jnp.int32(0), nblocks, block_step, (outputs, input_grads, s...]
    dot_general x12 -> x0, matrix products: 17.2 us -> none  [the longest x2 5.27 us: expert_block(): project = jnp.dot(inputs, gate_up, preferred_element_type=jnp.float32)]
    dynamic_update_slice x4 -> x0, local copies, waits for them, and re-layouts: 15.2 us -> none  [the longest x2 7.62 us: block_step(): lax.dynamic_update_slice_in_dim(input_grads, input_grad, row_begin, 0)]
    another operation x2 -> x0, other arithmetic: 14.6 us -> none  [the longest x1 14.5 us: local(): reduced = reduce_grads(jnp.stack(pieces, axis=1))]
  transfers between devices with their start and end apart: 3 -> 0, of which waited for: 3 -> 0; matrix products, arithmetic and copies ran while one was open for 1% -> 0% of each run, Pallas kernels for 0% -> 0%
where the time goes in v1:
time: 162 us; the launch traced here: 161 us
  Pallas kernels  150 us (93%)
  local copies, waits for them, and re-layouts  11.1 us (7%)
    pallas_call x1, Pallas kernels, local(): pl.pallas_call(kernel, out_shape=(jax.ShapeDtypeStruct((rows, model), BF1...  150 us
    unnamed x8, local copies, waits for them, and re-layouts  11.1 us

profile of v1, /device:TPU:0, one launch (start us, length us, event | category | flops | bytes accessed | tf_op | source)
XLA Modules:
  0.0 161.4 jit_solution(14010076838663862206)
XLA Ops:
  0.6 2.4 %copy.10 = bf16[256,2,1152]{2,0,1:T(8,128)(2,1)} copy(bf16[256,2,1152]{2,1,0:T(2,128)(2,1)} %param.7) | data formatting | bytes 2359296 | tf_op args[3]
  3.0 149.7 %shard_map.67 = (bf16[512,2048]{1,0:T(8,128)(2,1)}, bf16[512,2048]{1,0:T(8,128)(2,1)}, f32[2,256,1152]{2,1,0:T(8,128)}) custom-call(s32[1,2]{1,0:T(1,128)} %counts_ref.1, bf16[512,2048]{1,0:T(8,128)(2,1)} %x_ref.1, bf16[512,2048]{1,0:T(8,128)(2,1)} %dy_ref.1, bf16[2,256,1152]{2,1,0:T(8,128)(2,1)} %bitcast.5), custom_call_target="tpu_custom_call" | custom-call | flops 28991029248 | bytes 33554432 | tf_op jit(solution)/shard_map/pallas_call | solution.py:296
  152.7 0.0 copy-start.1
  152.7 5.0 %copy.8 = f32[256,2,1152]{2,1,0:T(2,128)} copy(f32[256,2,1152]{2,0,1:T(8,128)} %bitcast.4) | data formatting | bytes 4718592
  157.8 0.0 copy-done.1
  157.8 0.0 copy-start
  157.8 1.3 copy.13
  159.1 1.0 copy-done
  160.1 1.3 copy.14
Async XLA Ops:
  152.7 5.1 %copy-start.1 = (bf16[512,2048]{1,0:T(8,128)(2,1)S(1)}, bf16[512,2048]{1,0:T(8,128)(2,1)}, u32[]{:S(2)}) copy-start(bf16[512,2048]{1,0:T(8,128)(2,1)} %get-tuple-element.15) | copy-start | bytes 6291460
  157.8 2.3 %copy-start = (bf16[512,2048]{1,0:T(8,128)(2,1)S(1)}, bf16[512,2048]{1,0:T(8,128)(2,1)}, u32[]{:S(2)}) copy-start(bf16[512,2048]{1,0:T(8,128)(2,1)} %get-tuple-element.16) | copy-start | bytes 6291460

commit v2 on v1

v2 whole, which is shorter than its diff:
```python
import functools

import jax
import jax.numpy as jnp
from jax import lax
from jax.experimental import pallas as pl
from jax.experimental.pallas import tpu as pltpu
from jax.sharding import PartitionSpec as P

BLOCK = 128
INNER = 8
MESH = pl.DeviceIdType.MESH
BF16, F32 = jnp.bfloat16, jnp.float32


def flip(index, bit):
    return index + bit - 2 * bit * lax.rem(lax.div(index, bit), 2)


def dot(a, b, dims):
    return lax.dot_general(a, b, (dims, ((), ())), preferred_element_type=F32)


NN, NT, TN = ((1,), (0,)), ((1,), (1,)), ((0,), (0,))


def kernel(
    counts_ref, x_ref, dy_ref, w_ref,
    out_ref, grad_ref, wg_ref,
    w_all, pre, hgrad, ops,
    core_out, core_in, first_out, first_in, second_out, second_in, acc,
    z_out, z_in, z_peer, z_fin,
    w_sem, ag_send, ag_recv, core_send, core_recv, xy_send, xy_recv, z_send, z_recv,
):
    rows = x_ref.shape[0]
    experts, feat, width = w_ref.shape
    ff = width // 3
    shard = lax.axis_index("shard")
    rep = lax.axis_index("rep")
    local = lax.rem(shard, INNER)
    to_core, to_x, to_y = ((flip(shard, b), rep) for b in (1, 2, 4))
    z_pair, z_mirror = (shard, flip(rep, 1)), (shard, 3 - rep)
    inner_z = jnp.logical_or(rep == 1, rep == 2)
    partner = flip(local, 1)
    near = [local, flip(local, 2), flip(local, 4), flip(flip(local, 2), 4)]
    far = [partner, flip(partner, 2), flip(partner, 4), flip(flip(partner, 2), 4)]

    load = pltpu.make_async_copy(w_ref, w_all.at[local], w_sem)
    load.start()
    barrier = pltpu.get_barrier_semaphore()
    for other in (to_core, to_x, to_y, z_pair, z_mirror):
        pl.semaphore_signal(barrier, inc=1, device_id=other, device_id_type=MESH)
    load.wait()
    pl.semaphore_wait(barrier, 5)

    ex = lax.rem(rep, 2)
    ey = 1 - ex

    def share(k, member, e, device):
        block = w_all.at[member, e]
        return pltpu.make_async_remote_copy(
            src_ref=block, dst_ref=block, send_sem=ag_send.at[k], recv_sem=ag_recv.at[k],
            device_id=device, device_id_type=MESH,
        )

    over_x, over_y = share(0, near[0], ex, to_x), share(1, near[0], ey, to_y)
    on_y, on_x = share(2, near[1], ex, to_y), share(3, near[2], ey, to_x)
    pair_x, pair_y = share(4, near[1], ex, z_pair), share(5, near[2], ey, z_pair)
    held = [
        (0, 0), (0, 1), (1, ex), (2, ey), (1, ey), (2, ex), (3, ex), (3, ey),
    ]
    cross = [share(6 + k, near[d], e, to_core) for k, (d, e) in enumerate(held)]
    over_x.start()
    over_y.start()
    cross[0].start()
    cross[1].start()

    def span(e):
        padded = lax.div(counts_ref[0, 0] + (BLOCK - 1), BLOCK) * BLOCK
        begin = e * padded
        return begin, begin + counts_ref[0, e]

    def columns(member):
        return pl.ds(pl.multiple_of(member * feat, 128), feat)

    def project(member, e, first=False):
        position = lax.broadcasted_iota(jnp.int32, (rows, 1), 0)
        begin, end = span(e)
        keep = (position >= begin) & (position < end)
        x = x_ref[:, columns(member)]
        dy = dy_ref[:, columns(member)]
        zero = jnp.zeros_like(x)
        p = dot(jnp.where(keep, x, zero), w_all[member, e, :, : 2 * ff], NN)
        h = dot(jnp.where(keep, dy, zero), w_all[member, e, :, 2 * ff :], NN)
        if first:
            pre[...] = p
            hgrad[...] = h
        else:
            pre[...] += p
            hgrad[...] += h

    project(near[0], 0, True)
    project(near[0], 1)
    cross[0].wait_recv()
    cross[1].wait_recv()
    project(far[0], 0)
    project(far[0], 1)
    over_x.wait_recv()
    on_y.start()
    pair_x.start()
    cross[2].start()
    over_y.wait_recv()
    on_x.start()
    pair_y.start()
    cross[3].start()
    project(near[1], ex)
    project(near[2], ey)
    cross[2].wait_recv()
    project(far[1], ex)
    cross[3].wait_recv()
    project(far[2], ey)
    for k, copy in ((4, pair_x), (5, pair_y), (6, on_y), (7, on_x)):
        copy.wait_recv()
        cross[k].start()
    for d, e in held[4:]:
        project(near[d], e)
    for k in range(4, 8):
        cross[k].wait_recv()
        project(far[held[k][0]], held[k][1])

    def activate(i, carry):
        at = pl.ds(pl.multiple_of(i * BLOCK, BLOCK), BLOCK)
        a, b, g = pre[at, :ff], pre[at, ff:], hgrad[at, :]
        s = jax.nn.sigmoid(a)
        active = a * s
        values = (
            (g * b * s * (1.0 + a * (1.0 - s))).astype(BF16),
            (g * active).astype(BF16),
            (active * b).astype(BF16),
        )
        place = lax.broadcasted_iota(jnp.int32, (BLOCK, 1), 0) + i * BLOCK
        for e in range(experts):
            begin, end = span(e)
            keep = (place >= begin) & (place < end)
            for part, value in enumerate(values):
                ops[part, at, e * ff : (e + 1) * ff] = jnp.where(
                    keep, value, jnp.zeros_like(value)
                )
        return carry

    lax.fori_loop(0, rows // BLOCK, activate, 0)

    parts = 3

    def terms(member, part):
        source = dy_ref if part == 2 else x_ref
        return dot(source[:, columns(member)], ops[part], TN)

    def swap(part, d):
        return pltpu.make_async_remote_copy(
            src_ref=core_out.at[part, d], dst_ref=core_in.at[part, d],
            send_sem=core_send.at[part, d], recv_sem=core_recv.at[part, d],
            device_id=to_core, device_id_type=MESH,
        )

    def to_partner(part, d):
        core_out[part, d] = terms(far[d], part).astype(BF16)
        swap(part, d).start()

    def own_terms(part, d):
        value = terms(near[d], part)
        swap(part, d).wait_recv()
        value = value + core_in[part, d].astype(F32)
        return value[:, :ff], value[:, ff:]

    def step(part, k, src, dst, device):
        return pltpu.make_async_remote_copy(
            src_ref=src, dst_ref=dst, send_sem=xy_send.at[part, k], recv_sem=xy_recv.at[part, k],
            device_id=device, device_id_type=MESH,
        )

    first = [
        [step(p, k, first_out.at[p, k], first_in.at[p, k], (to_x, to_y)[k % 2]) for k in range(4)]
        for p in range(parts)
    ]
    second = [
        [step(p, 4 + k, second_out.at[p, k], second_in.at[p, k], (to_y, to_x)[k]) for k in range(2)]
        for p in range(parts)
    ]

    def send_first(part, k, value):
        first_out[part, k] = value.astype(BF16)
        first[part][k].start()

    def begin(part):
        to_partner(part, 3)
        to_partner(part, 1)
        zero, one = own_terms(part, 3)
        send_first(part, 0, zero)
        send_first(part, 1, one)
        to_partner(part, 2)
        zero, one = own_terms(part, 1)
        send_first(part, 2, zero)
        acc[part, 1] = one
        to_partner(part, 0)
        zero, one = own_terms(part, 2)
        send_first(part, 3, one)
        acc[part, 0] = zero
        zero, one = own_terms(part, 0)
        acc[part, 2] = zero
        acc[part, 3] = one

    def turn(part):
        for k in range(2):
            first[part][k].wait_recv()
            second_out[part, k] = (acc[part, k] + first_in[part, k].astype(F32)).astype(BF16)
            second[part][k].start()

    def hop(j, part, e, src, dst, device):
        return pltpu.make_async_remote_copy(
            src_ref=src.at[part, e], dst_ref=dst.at[part, e],
            send_sem=z_send.at[j, part, e], recv_sem=z_recv.at[j, part, e],
            device_id=device, device_id_type=MESH,
        )

    pieces = [(p, e) for p in range(parts) for e in range(experts)]
    inward = {k: hop(0, *k, z_out, z_in, z_pair) for k in pieces}
    across = {k: hop(1, *k, z_out, z_peer, z_mirror) for k in pieces}
    outward = {k: hop(2, *k, z_fin, z_fin, z_pair) for k in pieces}

    def enter(part):
        for e in range(experts):
            first[part][2 + e].wait_recv()
            second[part][e].wait_recv()
            total = (
                acc[part, 2 + e]
                + first_in[part, 2 + e].astype(F32)
                + second_in[part, e].astype(F32)
            )

            @pl.when(jnp.logical_not(inner_z))
            def _():
                z_out[part, e] = total.astype(BF16)
                inward[part, e].start()

            @pl.when(inner_z)
            def _():
                acc[part, 2 + e] = total

    def meet(part):
        @pl.when(inner_z)
        def _():
            for e in range(experts):
                inward[part, e].wait_recv()
                z_out[part, e] = (acc[part, 2 + e] + z_in[part, e].astype(F32)).astype(BF16)
                across[part, e].start()

    def leave(part):
        @pl.when(inner_z)
        def _():
            for e in range(experts):
                across[part, e].wait_recv()
                z_fin[part, e] = (
                    z_out[part, e].astype(F32) + z_peer[part, e].astype(F32)
                ).astype(BF16)
                outward[part, e].start()
                wg_ref[e, :, part * ff : (part + 1) * ff] = z_fin[part, e].astype(F32)

    def finish(part):
        @pl.when(jnp.logical_not(inner_z))
        def _():
            for e in range(experts):
                outward[part, e].wait_recv()
                wg_ref[e, :, part * ff : (part + 1) * ff] = z_fin[part, e].astype(F32)

    def rows_of(member, carry):
        at = columns(member)

        def both(part):
            cols = slice(part * ff, (part + 1) * ff)
            return jnp.concatenate([w_all[member, e, :, cols] for e in range(experts)], axis=1)

        out_ref[:, at] = dot(ops[2], both(2), NT).astype(BF16)
        grad_ref[:, at] = (dot(ops[0], both(0), NT) + dot(ops[1], both(1), NT)).astype(BF16)
        return carry

    begin(0)
    turn(0)
    begin(1)
    enter(0)
    turn(1)
    begin(2)
    meet(0)
    enter(1)
    turn(2)
    leave(0)
    lax.fori_loop(0, INNER // 2, rows_of, 0)
    meet(1)
    leave(1)
    enter(2)
    meet(2)
    lax.fori_loop(INNER // 2, INNER, rows_of, 0)
    leave(2)
    for part in range(parts):
        finish(part)

    @pl.when(inner_z)
    def _():
        for k in pieces:
            across[k].wait_send()
            outward[k].wait_send()

    @pl.when(jnp.logical_not(inner_z))
    def _():
        for k in pieces:
            inward[k].wait_send()

    for copy in [over_x, over_y, on_x, on_y, pair_x, pair_y] + cross:
        copy.wait_send()
    for part in range(parts):
        for copy in first[part] + second[part] + [swap(part, d) for d in range(4)]:
            copy.wait_send()


def local(spread, rows_in, cotangent, expert_counts, weights):
    rows, model = rows_in.shape
    own, experts, width = weights.shape
    ff = width // 3
    feat = own * spread

    def regroup(v, a, b):
        return v if spread == 1 else v.reshape(rows, a, b, own).swapaxes(1, 2).reshape(rows, model)

    w = weights.swapaxes(0, 1)
    if spread > 1:
        peers = [[h * INNER + m for h in range(spread)] for m in range(INNER)]
        w = lax.all_gather(w, "shard", axis=1, tiled=True, axis_index_groups=peers)

    vmem = pl.BlockSpec(memory_space=pltpu.VMEM)
    dma = pltpu.SemaphoreType.DMA
    block = (feat, width)
    rows_out, rows_grad, wg = pl.pallas_call(
        kernel,
        out_shape=(
            jax.ShapeDtypeStruct((rows, model), BF16),
            jax.ShapeDtypeStruct((rows, model), BF16),
            jax.ShapeDtypeStruct((experts, feat, width), F32),
        ),
        in_specs=[
            pl.BlockSpec(memory_space=pltpu.SMEM), vmem, vmem,
            pl.BlockSpec(memory_space=pl.ANY),
        ],
        out_specs=(vmem, vmem, vmem),
        scratch_shapes=[
            pltpu.VMEM((INNER, experts, *block), BF16),
            pltpu.VMEM((rows, 2 * ff), F32),
            pltpu.VMEM((rows, ff), F32),
            pltpu.VMEM((3, rows, experts * ff), BF16),
            pltpu.VMEM((3, 4, feat, experts * ff), BF16),
            pltpu.VMEM((3, 4, feat, experts * ff), BF16),
            pltpu.VMEM((3, 4, feat, ff), BF16),
            pltpu.VMEM((3, 4, feat, ff), BF16),
            pltpu.VMEM((3, 2, feat, ff), BF16),
            pltpu.VMEM((3, 2, feat, ff), BF16),
            pltpu.VMEM((3, 4, feat, ff), F32),
            pltpu.VMEM((3, experts, feat, ff), BF16),
            pltpu.VMEM((3, experts, feat, ff), BF16),
            pltpu.VMEM((3, experts, feat, ff), BF16),
            pltpu.VMEM((3, experts, feat, ff), BF16),
            dma,
            dma((14,)), dma((14,)),
            dma((3, 4)), dma((3, 4)),
            dma((3, 6)), dma((3, 6)),
            dma((3, 3, experts)), dma((3, 3, experts)),
        ],
        compiler_params=pltpu.CompilerParams(
            collective_id=0, has_side_effects=True, vmem_limit_bytes=62 * 1024 * 1024 - 1024 * 1024
        ),
        cost_estimate=pl.CostEstimate(
            flops=12 * rows * model * experts * width // 3 * 3, bytes_accessed=32 << 20,
            transcendentals=rows * ff,
        ),
    )(expert_counts, regroup(rows_in, spread, INNER), regroup(cotangent, spread, INNER), w)
    if spread > 1:
        wg = lax.psum_scatter(
            wg, "shard", scatter_dimension=1, tiled=True, axis_index_groups=peers
        )
    return regroup(rows_out, INNER, spread), regroup(rows_grad, INNER, spread), wg.swapaxes(0, 1)


def solution(mesh):
    rows_spec = P(("shard", "rep"), None)
    weight_spec = P("shard", None, None)
    return jax.shard_map(
        functools.partial(local, mesh.shape["shard"] // INNER),
        mesh=mesh,
        in_specs=(rows_spec, rows_spec, rows_spec, weight_spec),
        out_specs=(rows_spec, rows_spec, weight_spec),
        check_vma=False,
    )
```

time: 162 us -> 135 us (0.83)
  Pallas kernels: 150 us -> 123 us
    pallas_call x1, Pallas kernels: 150 us -> 123 us  [local(): pl.pallas_call(kernel, out_shape=(jax.ShapeDtypeStruct((rows, model), BF1...]
where the time goes in v2:
time: 135 us; the launch traced here: 134 us
  Pallas kernels  123 us (91%)
  local copies, waits for them, and re-layouts  11.1 us (8%)
    pallas_call x1, Pallas kernels, local(): pl.pallas_call(kernel, out_shape=(jax.ShapeDtypeStruct((rows, model), BF1...  123 us
    unnamed x8, local copies, waits for them, and re-layouts  11.1 us

profile of v2, /device:TPU:0, one launch (start us, length us, event | category | flops | bytes accessed | tf_op | source)
XLA Modules:
  0.0 134.3 jit_solution(1501889846651439261)
XLA Ops:
  0.6 2.4 %copy.10 = bf16[256,2,1152]{2,0,1:T(8,128)(2,1)} copy(bf16[256,2,1152]{2,1,0:T(2,128)(2,1)} %param.7) | data formatting | bytes 2359296 | tf_op args[3]
  3.0 122.6 %shard_map.67 = (bf16[512,2048]{1,0:T(8,128)(2,1)}, bf16[512,2048]{1,0:T(8,128)(2,1)}, f32[2,256,1152]{2,1,0:T(8,128)}) custom-call(s32[1,2]{1,0:T(1,128)} %counts_ref.1, bf16[512,2048]{1,0:T(8,128)(2,1)} %x_ref.1, bf16[512,2048]{1,0:T(8,128)(2,1)} %dy_ref.1, bf16[2,256,1152]{2,1,0:T(8,128)(2,1)} %bitcast.5), custom_call_target="tpu_custom_call" | custom-call | flops 28991029248 | bytes 33554432 | tf_op jit(solution)/shard_map/pallas_call | solution.py:342
  125.6 0.0 copy-start.1
  125.6 5.0 %copy.8 = f32[256,2,1152]{2,1,0:T(2,128)} copy(f32[256,2,1152]{2,0,1:T(8,128)} %bitcast.4) | data formatting | bytes 4718592
  130.7 0.0 copy-done.1
  130.7 0.0 copy-start
  130.7 1.3 copy.13
  132.0 1.0 copy-done
  133.0 1.3 copy.14
Async XLA Ops:
  125.6 5.1 %copy-start.1 = (bf16[512,2048]{1,0:T(8,128)(2,1)S(1)}, bf16[512,2048]{1,0:T(8,128)(2,1)}, u32[]{:S(2)}) copy-start(bf16[512,2048]{1,0:T(8,128)(2,1)} %get-tuple-element.15) | copy-start | bytes 6291460
  130.7 2.3 %copy-start = (bf16[512,2048]{1,0:T(8,128)(2,1)S(1)}, bf16[512,2048]{1,0:T(8,128)(2,1)}, u32[]{:S(2)}) copy-start(bf16[512,2048]{1,0:T(8,128)(2,1)} %get-tuple-element.16) | copy-start | bytes 6291460

commit v3 on v2

--- a/solution.py
+++ b/solution.py
@@ -25,12 +25,12 @@
 
 
 def kernel(
-    counts_ref, x_ref, dy_ref, w_ref,
-    out_ref, grad_ref, wg_ref,
-    w_all, pre, hgrad, ops,
+    counts_ref, x_hbm, dy_hbm, w_ref,
+    out_hbm, grad_hbm, wg_ref,
+    x_ref, dy_ref, out_ref, grad_ref, w_all, pre, hgrad, ops,
     core_out, core_in, first_out, first_in, second_out, second_in, acc,
     z_out, z_in, z_peer, z_fin,
-    w_sem, ag_send, ag_recv, core_send, core_recv, xy_send, xy_recv, z_send, z_recv,
+    w_sem, row_sem, ag_send, ag_recv, core_send, core_recv, xy_send, xy_recv, z_send, z_recv,
 ):
     rows = x_ref.shape[0]
     experts, feat, width = w_ref.shape
@@ -47,6 +47,10 @@
 
     load = pltpu.make_async_copy(w_ref, w_all.at[local], w_sem)
     load.start()
+    loads = [
+        pltpu.make_async_copy(x_hbm, x_ref, row_sem.at[0]),
+        pltpu.make_async_copy(dy_hbm, dy_ref, row_sem.at[1]),
+    ]
     barrier = pltpu.get_barrier_semaphore()
     for other in (to_core, to_x, to_y, z_pair, z_mirror):
         pl.semaphore_signal(barrier, inc=1, device_id=other, device_id_type=MESH)
@@ -74,6 +78,8 @@
     over_y.start()
     cross[0].start()
     cross[1].start()
+    for copy in loads:
+        copy.start()
 
     def span(e):
         padded = lax.div(counts_ref[0, 0] + (BLOCK - 1), BLOCK) * BLOCK
@@ -99,6 +105,8 @@
             pre[...] += p
             hgrad[...] += h
 
+    for copy in loads:
+        copy.wait()
     project(near[0], 0, True)
     project(near[0], 1)
     cross[0].wait_recv()
@@ -264,14 +272,14 @@
                     z_out[part, e].astype(F32) + z_peer[part, e].astype(F32)
                 ).astype(BF16)
                 outward[part, e].start()
-                wg_ref[e, :, part * ff : (part + 1) * ff] = z_fin[part, e].astype(F32)
+                wg_ref[e, :, part * ff : (part + 1) * ff] = z_fin[part, e]
 
     def finish(part):
         @pl.when(jnp.logical_not(inner_z))
         def _():
             for e in range(experts):
                 outward[part, e].wait_recv()
-                wg_ref[e, :, part * ff : (part + 1) * ff] = z_fin[part, e].astype(F32)
+                wg_ref[e, :, part * ff : (part + 1) * ff] = z_fin[part, e]
 
     def rows_of(member, carry):
         at = columns(member)
@@ -300,6 +308,12 @@
     enter(2)
     meet(2)
     lax.fori_loop(INNER // 2, INNER, rows_of, 0)
+    stores = [
+        pltpu.make_async_copy(out_ref, out_hbm, row_sem.at[2]),
+        pltpu.make_async_copy(grad_ref, grad_hbm, row_sem.at[3]),
+    ]
+    for copy in stores:
+        copy.start()
     leave(2)
     for part in range(parts):
         finish(part)
@@ -315,6 +329,8 @@
         for k in pieces:
             inward[k].wait_send()
 
+    for copy in stores:
+        copy.wait()
     for copy in [over_x, over_y, on_x, on_y, pair_x, pair_y] + cross:
         copy.wait_send()
     for part in range(parts):
@@ -337,6 +353,7 @@
         w = lax.all_gather(w, "shard", axis=1, tiled=True, axis_index_groups=peers)
 
     vmem = pl.BlockSpec(memory_space=pltpu.VMEM)
+    hbm = pl.BlockSpec(memory_space=pl.ANY)
     dma = pltpu.SemaphoreType.DMA
     block = (feat, width)
     rows_out, rows_grad, wg = pl.pallas_call(
@@ -344,14 +361,13 @@
         out_shape=(
             jax.ShapeDtypeStruct((rows, model), BF16),
             jax.ShapeDtypeStruct((rows, model), BF16),
-            jax.ShapeDtypeStruct((experts, feat, width), F32),
+            jax.ShapeDtypeStruct((experts, feat, width), BF16),
         ),
         in_specs=[
-            pl.BlockSpec(memory_space=pltpu.SMEM), vmem, vmem,
-            pl.BlockSpec(memory_space=pl.ANY),
+            pl.BlockSpec(memory_space=pltpu.SMEM), hbm, hbm, hbm,
         ],
-        out_specs=(vmem, vmem, vmem),
-        scratch_shapes=[
+        out_specs=(hbm, hbm, vmem),
+        scratch_shapes=[pltpu.VMEM((rows, model), BF16)] * 4 + [
             pltpu.VMEM((INNER, experts, *block), BF16),
             pltpu.VMEM((rows, 2 * ff), F32),
             pltpu.VMEM((rows, ff), F32),
@@ -368,6 +384,7 @@
             pltpu.VMEM((3, experts, feat, ff), BF16),
             pltpu.VMEM((3, experts, feat, ff), BF16),
             dma,
+            dma((4,)),
             dma((14,)), dma((14,)),
             dma((3, 4)), dma((3, 4)),
             dma((3, 6)), dma((3, 6)),
@@ -381,6 +398,7 @@
             transcendentals=rows * ff,
         ),
     )(expert_counts, regroup(rows_in, spread, INNER), regroup(cotangent, spread, INNER), w)
+    wg = wg.astype(F32)
     if spread > 1:
         wg = lax.psum_scatter(
             wg, "shard", scatter_dimension=1, tiled=True, axis_index_groups=peers

time: 135 us -> 131 us (0.970)
  Pallas kernels: 123 us -> 120 us
  local copies, waits for them, and re-layouts: 11.1 us -> 9.3 us
  other arithmetic: 0 us -> 1.43 us
    pallas_call x1, Pallas kernels: 123 us -> 120 us  [local(): pl.pallas_call(kernel, out_shape=(jax.ShapeDtypeStruct((rows, model), BF1...]
    unnamed x8, local copies, waits for them, and re-layouts: 11.1 us -> 9.3 us
    transpose x0 -> x1, other arithmetic: none -> 1.43 us  [local(): wg.swapaxes(0, 1)]
where the time goes in v3:
time: 131 us
  Pallas kernels  120 us (92%)
  local copies, waits for them, and re-layouts  9.3 us (7%)
  other arithmetic  1.43 us (1%)
    pallas_call x1, Pallas kernels, local(): pl.pallas_call(kernel, out_shape=(jax.ShapeDtypeStruct((rows, model), BF1...  120 us
    unnamed x8, local copies, waits for them, and re-layouts  9.3 us

profile of v3, /device:TPU:0, one launch (start us, length us, event | category | flops | bytes accessed | tf_op | source)
XLA Modules:
  0.0 131.0 jit_solution(9951120741101814272)
XLA Ops:
  0.6 2.4 %copy.10 = bf16[256,2,1152]{2,0,1:T(8,128)(2,1)} copy(bf16[256,2,1152]{2,1,0:T(2,128)(2,1)} %param.7) | data formatting | bytes 2359296 | tf_op args[3]
  3.0 119.6 %shard_map.67 = (bf16[512,2048]{1,0:T(8,128)(2,1)}, bf16[512,2048]{1,0:T(8,128)(2,1)}, bf16[2,256,1152]{2,1,0:T(8,128)(2,1)}) custom-call(s32[1,2]{1,0:T(1,128)} %counts_ref.1, bf16[512,2048]{1,0:T(8,128)(2,1)} %x_hbm.1, bf16[512,2048]{1,0:T(8,128)(2,1)} %dy_hbm.1, bf16[2,256,1152]{2,1,0:T(8,128)(2,1)} %bitcast.5), custom_call_target="tpu_custom_call" | custom-call | flops 28991029248 | bytes 33554432 | tf_op jit(solution)/shard_map/pallas_call | solution.py:359
  122.6 1.4 %convert_bitcast_fusion = f32[256,2,1152]{2,0,1:T(8,128)S(1)} fusion(bf16[2,256,1152]{2,1,0:T(8,128)(2,1)} %get-tuple-element.8), kind=kLoop, calls=%fused_computation | loop fusion | flops 589824 | bytes 3538944 | tf_op jit(solution)/shard_map/transpose | solution.py:406
  124.1 0.0 copy-start.1
  124.1 3.2 %copy.8 = f32[256,2,1152]{2,1,0:T(2,128)} copy(f32[256,2,1152]{2,0,1:T(8,128)S(1)} %convert_bitcast_fusion) | data formatting | bytes 4718592
  127.3 0.0 copy-done.1
  127.3 0.0 copy-start
  127.3 1.3 %copy.13 = bf16[512,2048]{1,0:T(8,128)(2,1)} copy(bf16[512,2048]{1,0:T(8,128)(2,1)S(1)} %copy-done.1) | data formatting | bytes 4194304
  128.6 1.0 copy-done
  129.7 1.3 %copy.14 = bf16[512,2048]{1,0:T(8,128)(2,1)} copy(bf16[512,2048]{1,0:T(8,128)(2,1)S(1)} %copy-done) | data formatting | bytes 4194304
Async XLA Ops:
  124.1 3.2 %copy-start.1 = (bf16[512,2048]{1,0:T(8,128)(2,1)S(1)}, bf16[512,2048]{1,0:T(8,128)(2,1)}, u32[]{:S(2)}) copy-start(bf16[512,2048]{1,0:T(8,128)(2,1)} %get-tuple-element.15) | copy-start | bytes 6291460
  127.3 2.3 %copy-start = (bf16[512,2048]{1,0:T(8,128)(2,1)S(1)}, bf16[512,2048]{1,0:T(8,128)(2,1)}, u32[]{:S(2)}) copy-start(bf16[512,2048]{1,0:T(8,128)(2,1)} %get-tuple-element.16) | copy-start | bytes 6291460
